TPU v7x, 512 devices: a whole 4x8x8 slice. The times are simulated.
512 devices in a mesh: frame: 32 (over y_hi, x, core), space: 16 (over z, y_lo).
Axes of the slice: x: 4, y: 8 (y_hi: 4, y_lo: 2; y = y_hi * 2 + y_lo), z: 8, core: 2. Of those that a mesh axis runs over, the one named last changes fastest.
Arguments:
- current_image: float32 [64, 16, 160, 2, 160], P('frame', 'space'), may hold values from -6 to 6
- coil_maps: bfloat16 [16, 8, 160, 2, 160], P('space'), may hold values from -2 to 2
- measured_lines: float32 [64, 16, 8, 40, 2, 160], P('frame', 'space'), may hold values from -6 to 6
- sampled_lines: int32 [64, 40], P('frame'), may hold values from 0 to 159, as said below
- prior_weights: float32 [64], replicated, may hold values from 0.2 to 2
- langevin_noise: float32 [64, 16, 160, 2, 160], P('frame', 'space'), may hold values from -2 to 2
Outputs:
- next_image: float32 [64, 16, 160, 2, 160], P('frame', 'space')
Inputs may be any that keep to these rules, and one draw needn't show every extreme that they name: `sampled_lines`: each frame's 40 indices are distinct and include 0 and 159, the lowest phase-encode frequencies.
All inputs are finite; a program needn't handle non-finite values.
Results may differ from a plain program's by a relative error of at most 0.005.
Values sent between devices are 32-bit elements; how exact they have to be, the bound alone decides.
A program may use at most 64 MiB of HBM per device.

v0:
```python
import math

import jax
import jax.numpy as jnp
from jax import lax
from jax.sharding import PartitionSpec as P

step_size = 0.5
coupling = 0.25
softness = 0.01


def with_halo(array, sides, width):
    for axis, dim in sides:
        count, length = (lax.axis_size(axis), array.shape[dim])
        up = [(i, (i + 1) % count) for i in range(count - 1)]
        down = [(j, i) for i, j in up]
        last = lax.slice_in_dim(array, length - width, length, axis=dim)
        initial = lax.slice_in_dim(array, 0, width, axis=dim)
        before = lax.ppermute(last, axis, up)
        after = lax.ppermute(initial, axis, down)
        array = jnp.concatenate([before, array, after], axis=dim)
    return array


def cosine_pair(waves, positions, count):
    product = waves[..., None] * positions % count
    angles = 2.0 * math.pi / count * product.astype(jnp.float32)
    scale = 1.0 / math.sqrt(count)
    return (jnp.cos(angles) * scale, jnp.sin(angles) * scale)


def row_table(count):
    indices = jnp.arange(count, dtype=jnp.int32)
    cosine, sine = cosine_pair(indices, indices, count)
    upper = jnp.concatenate([cosine, -sine], axis=1)
    lower = jnp.concatenate([sine, cosine], axis=1)
    return jnp.concatenate([upper, lower], axis=0).astype(jnp.bfloat16)


def line_table(waves, count):
    positions = jnp.arange(count, dtype=jnp.int32)
    cosine, sine = cosine_pair(waves, positions, count)
    real_part = jnp.stack([cosine, sine], axis=-1)
    imag_part = jnp.stack([-sine, cosine], axis=-1)
    return jnp.stack([real_part, imag_part], axis=-4)


def sense(maps, field):
    map_re = maps[:, :, :, 0, :].astype(jnp.float32)[None]
    map_im = maps[:, :, :, 1, :].astype(jnp.float32)[None]
    field_re = field[:, :, None, :, 0, :]
    field_im = field[:, :, None, :, 1, :]
    coil_real = map_re * field_re - map_im * field_im
    coil_imag = map_re * field_im + map_im * field_re
    return jnp.stack([coil_real, coil_imag], axis=4).astype(jnp.bfloat16)


def combine(maps, back_image):
    map_re = maps[:, :, :, 0, :].astype(jnp.float32)[None]
    map_im = maps[:, :, :, 1, :].astype(jnp.float32)[None]
    back_re = back_image[:, :, :, :, 0, :]
    back_im = back_image[:, :, :, :, 1, :]
    grad_re = jnp.sum(map_re * back_re + map_im * back_im, axis=2)
    grad_im = jnp.sum(map_re * back_im - map_im * back_re, axis=2)
    return jnp.stack([grad_re, grad_im], axis=3)


def on_device(
    current_image, coil_maps, measured_lines, sampled_lines, prior_weights, langevin_noise
):
    frames_dev, slices_dev, height, _, width = current_image.shape
    rotation = row_table(width)
    frame_tables = line_table(sampled_lines, height).astype(jnp.bfloat16)
    coil_image = sense(coil_maps, current_image)
    shape = coil_image.shape
    flat = coil_image.reshape(shape[:4] + (2 * width,))
    row_spectra = (
        jnp.dot(flat, rotation, preferred_element_type=jnp.float32)
        .astype(jnp.bfloat16)
        .reshape(shape)
    )
    estimate = jnp.einsum(
        "folxi,fscxiy->fscloy", frame_tables, row_spectra, preferred_element_type=jnp.float32
    )
    residual = (estimate - measured_lines).astype(jnp.bfloat16)
    back_rows = jnp.einsum(
        "folxi,fscloy->fscxiy", frame_tables, residual, preferred_element_type=jnp.float32
    )
    back_rows = back_rows.astype(jnp.bfloat16)
    back_image = jnp.dot(
        back_rows.reshape(shape[:4] + (2 * width,)), rotation.T, preferred_element_type=jnp.float32
    ).reshape(shape)
    data_grad = combine(coil_maps, back_image)
    total_frames = frames_dev * lax.axis_size("frame")
    time_table = line_table(jnp.arange(total_frames, dtype=jnp.int32), total_frames)
    spectrum = jnp.einsum(
        "okfi,fsxiy->ksxoy",
        time_table,
        lax.all_to_all(current_image, "frame", split_axis=2, concat_axis=0, tiled=True),
        precision=lax.Precision.HIGHEST,
    )
    magnitude = jnp.sqrt(spectrum[:, :, :, 0, :] ** 2 + spectrum[:, :, :, 1, :] ** 2 + softness)
    shrunk = prior_weights[:, None, None, None, None] * spectrum / magnitude[:, :, :, None, :]
    moved = jnp.einsum("okfi,ksxoy->fsxiy", time_table, shrunk, precision=lax.Precision.HIGHEST)
    prior_grad = lax.all_to_all(moved, "frame", split_axis=0, concat_axis=2, tiled=True)
    padded = with_halo(current_image, (("space", 1),), 1)
    slice_grad = coupling * (2.0 * current_image - padded[:, :-2] - padded[:, 2:])
    return current_image - step_size * (data_grad + prior_grad + slice_grad) + langevin_noise


def solution(mesh):
    return jax.shard_map(
        on_device,
        mesh=mesh,
        in_specs=(
            P("frame", "space", None, None, None),
            P("space", None, None, None, None),
            P("frame", "space", None, None, None, None),
            P("frame", None),
            P(),
            P("frame", "space", None, None, None),
        ),
        out_specs=P("frame", "space", None, None, None),
        check_vma=False,
    )
```

profile of v0, /device:TPU:201, one launch (start us, length us, event | category | flops | bytes accessed | tf_op | source)
XLA Modules:
  0.0 109.2 jit_solution(4588862148439000523)
XLA Ops:
  0.0 2.1 %copy.78 = f32[2,1,160,2,160]{4,2,0,3,1:T(8,128)} copy(f32[2,1,160,2,160]{4,3,2,1,0:T(2,128)} %param.6) | data formatting | bytes 819200 | tf_op args[0]
  2.1 5.1 %collective-permute-start = (f32[2,1,160,2,160]{4,2,0,3,1:T(8,128)}, f32[2,1,160,2,160]{4,2,0,3,1:T(8,128)}, u32[]{:S(2)}, u32[]{:S(2)}) collective-permute-start(f32[2,1,160,2,160]{4,2,0,3,1:T(8,128)} %copy.78), channel_id=1, source_target_pairs={{0,1},{1,2},{2,3},{3,4},{4,5},{5,6},{6,7},{7,8},{8,9},{9,10},{10,1... | collective-permute-start | bytes 1228808 | tf_op jit(solution)/shard_map/ppermute | solution.py:20
  7.2 1.9 %collective-permute-start.1 = (f32[2,1,160,2,160]{4,2,0,3,1:T(8,128)}, f32[2,1,160,2,160]{4,2,0,3,1:T(8,128)}, u32[]{:S(2)}, u32[]{:S(2)}) collective-permute-start(f32[2,1,160,2,160]{4,2,0,3,1:T(8,128)} %copy.78), channel_id=1, source_target_pairs={{1,0},{2,1},{3,2},{4,3},{5,4},{6,5},{7,6},{8,7},{9,8},{10,9},{11,1... | collective-permute-start | bytes 1228808 | tf_op jit(solution)/shard_map/ppermute | solution.py:21
  9.1 2.2 %copy.68 = f32[2,1,160,2,160]{4,3,1,0,2:T(2,128)} copy(f32[2,1,160,2,160]{4,3,2,1,0:T(2,128)} %param.6) | data formatting | bytes 819200 | tf_op args[0]
  11.3 10.7 %all-to-all-start = ((f32[2,1,160,2,160]{4,3,1,0,2:T(2,128)}), f32[2,1,160,2,160]{4,3,1,0,2:T(2,128)S(1)}, u32[]{:S(2)}, u32[]{:S(2)}) async-start(f32[2,1,160,2,160]{4,3,1,0,2:T(2,128)} %copy.68), calls=%async_computation | async-start | bytes 1310720 | tf_op jit(solution)/shard_map/all_to_all | solution.py:100
  22.0 1.1 %slice_bitcast_fusion.3 = (f32[2,160,160]{2,1,0:T(8,128)S(1)}, f32[2,160,160]{2,1,0:T(8,128)S(1)}) fusion(f32[2,1,160,2,160]{4,2,0,3,1:T(8,128)} %copy.78), kind=kLoop, calls=%fused_computation.37 | loop fusion | bytes 819200 | tf_op jit(solution)/shard_map/mul | solution.py:54
  23.1 0.7 negate_convert_fusion
  23.8 0.7 fusion.36
  24.4 0.8 sine_multiply_fusion.2
  25.2 0.8 fusion.53
  25.9 2.4 %fusion.57 = (bf16[1,8,160,1,160]{4,3,2,1,0:T(2,128)(2,1)S(1)}, bf16[1,8,160,1,160]{4,3,2,1,0:T(2,128)(2,1)S(1)}) fusion(bf16[1,8,160,2,160]{4,3,2,1,0:T(2,128)(2,1)S(1)} %copy-done.1), kind=kLoop, calls=%fused_computation.88 | loop fusion | bytes 1638400 | tf_op jit(solution)/shard_map/slice | solution.py:60
  28.5 5.5 %subtract_convert_fusion = (bf16[2,1,8,160,1,160]{5,4,3,2,0,1:T(2,128)(2,1)S(1)}, bf16[2,1,8,160,1,160]{5,4,3,2,0,1:T(2,128)(2,1)S(1)}) fusion(f32[2,160,160]{2,1,0:T(8,128)S(1)} %get-tuple-element.12, f32[8,160,160]{2,1,0:T(8,128)S(1)} %get-tuple-element.20, f32[2,160,160]{2,1,0:T(8,128)S(1)} %get-tuple-element.11, f32[8,160,160]{2,1,0:T(8,128)S(1)} %get-tuple-element.21), kind=kLoop, calls=%fused_computation.9 | loop fusion | flops 3276800 | bytes 3686400 | tf_op jit(solution)/shard_map/convert.16
  34.0 7.3 %pad_maximum_fusion = bf16[2,1,8,160,2,160]{5,4,3,2,0,1:T(2,128)(2,1)} fusion(bf16[2,1,8,160,1,160]{5,4,3,2,0,1:T(2,128)(2,1)S(1)} %get-tuple-element.8, bf16[2,1,8,160,1,160]{5,4,3,2,0,1:T(2,128)(2,1)S(1)} %get-tuple-element.7), kind=kLoop, calls=%fused_computation.3 | loop fusion | flops 3276800 | bytes 3276800 | tf_op jit(solution)/shard_map/stack | solution.py:56
  41.4 6.6 %convert_element_type.117 = bf16[2,8,160,320]{3,2,1,0:T(8,128)(2,1)} reshape(bf16[2,1,8,160,2,160]{5,4,3,2,0,1:T(2,128)(2,1)} %pad_maximum_fusion) | data formatting | bytes 3276800 | tf_op jit(solution)/shard_map/convert_element_type | solution.py:56
  48.0 4.3 %convolution_convert_fusion = bf16[2,8,160,320]{3,2,1,0:T(8,128)(2,1)} fusion(bf16[2,8,160,320]{3,2,1,0:T(8,128)(2,1)} %convert_element_type.117, bf16[160,160]{1,0:T(8,128)(2,1)S(1)} %get-tuple-element.23, bf16[160,160]{1,0:T(8,128)(2,1)S(1)} %fusion.36, bf16[160,160]{1,0:T(8,128)(2,1)S(1)} %get-tuple-element.22), kind=kOutput, calls=%fused_computation.11 | convolution fusion | flops 525926400 | bytes 3430400 | tf_op jit(solution)/shard_map/dot_general | solution.py:79
  52.3 0.7 maximum_bitcast_fusion.2
  52.9 7.0 %reshape.357 = bf16[2,8,160,2,160]{4,3,2,1,0:T(2,128)(2,1)} reshape(bf16[2,8,160,320]{3,2,1,0:T(8,128)(2,1)} %convolution_convert_fusion) | data formatting | bytes 3276800 | tf_op jit(solution)/shard_map/reshape.14
  60.0 1.1 %fusion.46 = (bf16[2,40,160,1]{2,1,3,0:T(8,128)(2,1)S(1)}, bf16[2,40,160,1]{2,1,3,0:T(8,128)(2,1)S(1)}, bf16[2,40,160,1]{2,1,3,0:T(8,128)(2,1)S(1)}) fusion(s32[2,40]{1,0:T(2,128)} %param.9), kind=kLoop, calls=%fused_computation.71 | loop fusion | flops 192000 | bytes 77120 | tf_op jit(solution)/shard_map/convert.9
  61.1 0.7 maximum_bitcast_fusion
  61.8 5.1 %bitcast_convert_fusion = bf16[2,8,160,160,2]{3,2,4,1,0:T(8,128)(2,1)} fusion(f32[2,1,8,40,2,160]{5,4,3,2,1,0:T(2,128)} %param.8, bf16[2,8,160,2,160,1]{4,3,2,1,0,5:T(2,128)(2,1)} %bitcast.148, bf16[2,1,40,160,2]{3,2,4,1,0:T(8,128)(2,1)} %get-tuple-element.14, bf16[2,1,40,160,2]{3,2,4,1,0:T(8,128)(2,1)} %get-tuple-element.13), kind=kOutput, calls=%fused_computation | convolution fusion | flops 263628800 | bytes 4198400 | tf_op jit(solution)/shard_map/folxi,fscloy->fscxiy/dot_general | solution.py:87
  66.9 1.2 %copy.141 = f32[2,1,32,5,2,160]{5,0,2,4,3,1:T(2,128)} copy(f32[2,1,32,5,2,160]{5,4,0,3,2,1:T(2,128)S(1)} %bitcast.149) | data formatting | bytes 819200 | tf_op jit(solution)/shard_map/all_to_all | solution.py:100
  68.0 1.5 %reshape.374 = f32[64,5,2,160,1]{3,0,2,1,4:T(8,128)S(1)} reshape(f32[32,2,1,5,2,160]{5,1,0,4,3,2:T(2,128)} %bitcast.150) | data formatting | bytes 819200 | tf_op jit(solution)/shard_map/reshape.23
  69.6 1.6 %convolution_bitcast_fusion.2 = f32[64,1,5,2,160]{4,0,2,3,1:T(8,128)S(1)} fusion(f32[64,5,2,160,1]{3,0,2,1,4:T(8,128)S(1)} %reshape.374, f32[1,64,64,2]{2,1,3,0:T(8,128)} %get-tuple-element.16, f32[1,64,64,2]{2,1,3,0:T(8,128)} %get-tuple-element.15), kind=kOutput, calls=%fused_computation.16 | convolution fusion | flops 157302784 | bytes 884736 | tf_op jit(solution)/shard_map/okfi,fsxiy->ksxoy/dot_general | solution.py:97
  71.3 1.7 %convolution_bitcast_fusion.1 = f32[64,1,5,2,160]{4,0,3,2,1:T(8,128)S(1)} fusion(f32[64,1,5,2,160]{4,0,2,3,1:T(8,128)S(1)} %convolution_bitcast_fusion.2, f32[64,5,160]{2,0,1:T(8,128)S(1)} %fusion.26, f32[64]{0:T(128)S(1)} %copy-done.4, f32[1,64,64,2]{2,1,3,0:T(8,128)} %get-tuple-element.16, f32[1,64,64,2]{2,1,3,0:T(8,128)} %get-tuple-element.15), kind=kOutput, calls=%fused_computation.15 | convolution fusion | flops 157507584 | bytes 1089792 | tf_op jit(solution)/shard_map/okfi,ksxoy->fsxiy/dot_general | solution.py:105
  73.0 1.4 %copy.72 = f32[64,1,5,2,160]{4,3,2,1,0:T(2,128)} copy(f32[64,1,5,2,160]{4,0,3,2,1:T(8,128)S(1)} %convolution_bitcast_fusion.1) | data formatting | bytes 819200 | tf_op jit(solution)/shard_map/okfi,ksxoy->fsxiy/transpose | solution.py:105
  74.4 9.8 %all-to-all-start.1 = ((f32[64,1,5,2,160]{4,3,2,1,0:T(2,128)}), f32[64,1,5,2,160]{4,3,2,1,0:T(2,128)}, u32[]{:S(2)}, u32[]{:S(2)}) async-start(f32[64,1,5,2,160]{4,3,2,1,0:T(2,128)} %copy.72), calls=%async_computation.1 | async-start | bytes 1310720 | tf_op jit(solution)/shard_map/all_to_all | solution.py:106
  84.4 4.0 %convolution_bitcast_fusion = f32[2,1,8,160,2,160]{5,3,4,2,0,1:T(8,128)S(1)} fusion(bf16[2,8,160,320,1]{2,3,4,1,0:T(8,128)(2,1)} %bitcast.147, bf16[2,160,320,1,1]{2,1,0,4,3:T(8,128)(2,1)S(1)} %bitcast.153), kind=kOutput, calls=%fused_computation.10 | convolution fusion | flops 524288000 | bytes 5120000 | tf_op jit(solution)/shard_map/dot_general | solution.py:91
  88.4 1.8 %add_reduce_fusion = (f32[2,160,160]{2,1,0:T(8,128)}, f32[2,160,160]{2,1,0:T(8,128)}) fusion(f32[2,1,8,160,2,160]{5,3,4,2,0,1:T(8,128)S(1)} %convolution_bitcast_fusion, f32[8,160,160]{2,1,0:T(8,128)S(1)} %get-tuple-element.20, f32[8,160,160]{2,1,0:T(8,128)S(1)} %get-tuple-element.21), kind=kLoop, calls=%fused_computation.7 | loop fusion | flops 3174400 | bytes 5324800 | tf_op jit(solution)/shard_map/reduce_sum | solution.py:64
  90.2 14.4 %all-to-all-done.1 = f32[64,1,5,2,160]{4,3,2,1,0:T(2,128)} async-done(((f32[64,1,5,2,160]{4,3,2,1,0:T(2,128)}), f32[64,1,5,2,160]{4,3,2,1,0:T(2,128)}, u32[]{:S(2)}, u32[]{:S(2)}) %all-to-all-start.1) | async-done | bytes 409632 | tf_op jit(solution)/shard_map/all_to_all | solution.py:106
  104.6 1.3 %copy.73 = f32[32,2,1,5,2,160]{5,4,3,0,1,2:T(2,128)S(1)} copy(f32[32,2,1,5,2,160]{5,4,3,1,0,2:T(2,128)} %bitcast.58) | data formatting | bytes 819200 | tf_op jit(solution)/shard_map/all_to_all | solution.py:106
  105.9 1.9 %fusion.19 = f32[2,1,160,2,160]{4,2,0,3,1:T(8,128)S(1)} fusion(f32[2,1,160,1,160]{4,2,0,3,1:T(8,128)} %bitcast.152, f32[2,1,160,1,160]{4,2,0,3,1:T(8,128)} %bitcast.151, f32[2,1,160,2,160]{4,3,2,1,0:T(2,128)} %param.11, f32[2,1,160,2,160]{4,3,2,0,1:T(2,128)S(1)} %bitcast.146, f32[2,1,160,2,160]{4,2,0,3,1:T(8,128)} %collective-permute-done.1, ...), kind=kLoop, calls=%fused_computation.22 | loop fusion | flops 1024000 | bytes 2867200 | tf_op jit(solution)/shard_map/add | solution.py:109
  107.9 1.3 %copy.80 = f32[2,1,160,2,160]{4,3,2,1,0:T(2,128)} copy(f32[2,1,160,2,160]{4,2,0,3,1:T(8,128)S(1)} %fusion.19) | data formatting | bytes 819200 | tf_op jit(solution)/shard_map/add | solution.py:109
  (16 shorter events, 0.5 us)
Async XLA Ops:
  0.0 25.9 %copy-start.1 = (bf16[1,8,160,2,160]{4,3,2,1,0:T(2,128)(2,1)S(1)}, bf16[1,8,160,2,160]{4,3,2,1,0:T(2,128)(2,1)}, u32[]{:S(2)}) copy-start(bf16[1,8,160,2,160]{4,3,2,1,0:T(2,128)(2,1)} %param.7) | copy-start | bytes 2457604
  2.1 103.8 %collective-permute-start = (f32[2,1,160,2,160]{4,2,0,3,1:T(8,128)}, f32[2,1,160,2,160]{4,2,0,3,1:T(8,128)}, u32[]{:S(2)}, u32[]{:S(2)}) collective-permute-start(f32[2,1,160,2,160]{4,2,0,3,1:T(8,128)} %copy.78), channel_id=1, source_target_pairs={{0,1},{1,2},{2,3},{3,4},{4,5},{5,6},{6,7},{7,8},{8,9},{9,10},{10,1... | collective-permute-start | bytes 1228808 | tf_op jit(solution)/shard_map/ppermute | solution.py:20
  7.2 98.7 %collective-permute-start.1 = (f32[2,1,160,2,160]{4,2,0,3,1:T(8,128)}, f32[2,1,160,2,160]{4,2,0,3,1:T(8,128)}, u32[]{:S(2)}, u32[]{:S(2)}) collective-permute-start(f32[2,1,160,2,160]{4,2,0,3,1:T(8,128)} %copy.78), channel_id=1, source_target_pairs={{1,0},{2,1},{3,2},{4,3},{5,4},{6,5},{7,6},{8,7},{9,8},{10,9},{11,1... | collective-permute-start | bytes 1228808 | tf_op jit(solution)/shard_map/ppermute | solution.py:21
  11.3 55.6 %all-to-all-start = ((f32[2,1,160,2,160]{4,3,1,0,2:T(2,128)}), f32[2,1,160,2,160]{4,3,1,0,2:T(2,128)S(1)}, u32[]{:S(2)}, u32[]{:S(2)}) async-start(f32[2,1,160,2,160]{4,3,1,0,2:T(2,128)} %copy.68), calls=%async_computation | async-start | bytes 1310720 | tf_op jit(solution)/shard_map/all_to_all | solution.py:100
  48.0 4.3 %copy-start.2 = (f32[64,64,1]{1,0,2:T(8,128)S(1)}, f32[64,64,1]{1,0,2:T(8,128)}, u32[]{:S(2)}) copy-start(f32[64,64,1]{1,0,2:T(8,128)} %get-tuple-element.25) | copy-start | bytes 49156
  48.0 4.3 %copy-start.3 = (f32[64,64,1]{1,0,2:T(8,128)S(1)}, f32[64,64,1]{1,0,2:T(8,128)}, u32[]{:S(2)}) copy-start(f32[64,64,1]{1,0,2:T(8,128)} %fusion.53) | copy-start | bytes 49156
  66.8 4.5 %copy-start.4 = (f32[64]{0:T(128)S(1)}, f32[64]{0:T(128)}, u32[]{:S(2)}) copy-start(f32[64]{0:T(128)} %param.10) | copy-start | bytes 772
  74.4 30.2 %all-to-all-start.1 = ((f32[64,1,5,2,160]{4,3,2,1,0:T(2,128)}), f32[64,1,5,2,160]{4,3,2,1,0:T(2,128)}, u32[]{:S(2)}, u32[]{:S(2)}) async-start(f32[64,1,5,2,160]{4,3,2,1,0:T(2,128)} %copy.72), calls=%async_computation.1 | async-start | bytes 1310720 | tf_op jit(solution)/shard_map/all_to_all | solution.py:106
  88.3 17.6 %copy-start = (f32[2,1,160,2,160]{4,3,2,1,0:T(2,128)S(1)}, f32[2,1,160,2,160]{4,3,2,1,0:T(2,128)}, u32[]{:S(2)}) copy-start(f32[2,1,160,2,160]{4,3,2,1,0:T(2,128)} %param.6) | copy-start | bytes 1228804
where the time goes:
time: 110 us; the launch traced here: 109 us
  local copies, waits for them, and re-layouts  28.1 us (26%)
  starting transfers between devices  27.5 us (25%)
  other arithmetic  22.4 us (20%)
  matrix products  16.7 us (15%)
  waiting for transfers between devices  14.4 us (13%)
    all_to_all x1, waiting for transfers between devices, on_device(): lax.all_to_all(moved, 'frame', split_axis=0, concat_axis=2, tiled=True)  14.4 us
    all_to_all x1, starting transfers between devices, on_device(): lax.all_to_all(current_image, 'frame', split_axis=2, concat_axis=0, tiled...  10.7 us
    all_to_all x1, starting transfers between devices, on_device(): lax.all_to_all(moved, 'frame', split_axis=0, concat_axis=2, tiled=True)  9.82 us
    another operation x2, local copies, waits for them, and re-layouts  8.55 us
    another operation x4, other arithmetic  7.95 us
    another operation x1, other arithmetic, sense(): return jnp.stack([coil_real, coil_imag], axis=4).astype(jnp.bfloat16)  7.31 us
    convert_element_type x1, local copies, waits for them, and re-layouts, sense(): return jnp.stack([coil_real, coil_imag], axis=4).astype(jnp.bfloat16)  6.64 us
    dot_general x1, matrix products, on_device(): jnp.einsum('folxi,fscloy->fscxiy', frame_tables, residual, preferred_elem...  5.09 us
  transfers between devices with their start and end apart: 4, of which 1 were waited for; matrix products, arithmetic and copies ran while one was open for 57% of the time, Pallas kernels for 0%

commit v1 on v0

v1 whole, which is shorter than its diff:
```python
import math

import jax
import jax.numpy as jnp
import ml_dtypes
import numpy as np
from jax import lax
from jax.experimental import pallas as pl
from jax.experimental.pallas import tpu as pltpu
from jax.sharding import PartitionSpec as P

MESH = pl.DeviceIdType.MESH
F32, BF16 = jnp.float32, jnp.bfloat16
ROWS = COLS = 160
COILS, LINES, FRAMES = 8, 40, 64
SOFTNESS = 0.01
MAIN = 128
GROUPS = 200
PEERS = 64
HALF = 32


def dft(count):
    index = np.arange(count)
    angles = 2.0 * math.pi / count * (index[:, None] * index[None, :] % count)
    return np.cos(angles) / math.sqrt(count), -np.sin(angles) / math.sqrt(count)


def row_tables():
    real, imag = dft(COLS)
    return np.stack([real, imag]).astype(np.float32).astype(ml_dtypes.bfloat16)


def time_tables():
    real, imag = dft(FRAMES)
    upper = np.stack([real, -imag], axis=-1).reshape(FRAMES, 2 * FRAMES)
    lower = np.stack([imag, real], axis=-1).reshape(FRAMES, 2 * FRAMES)
    forward = np.concatenate([upper, lower], axis=0)
    return np.stack([forward, forward.T]).astype(np.float32)


def dot(a, b):
    return jnp.dot(a, b, preferred_element_type=F32)


def exact_dot(a, b):
    return jnp.dot(a, b, precision=lax.Precision.HIGHEST, preferred_element_type=F32)


class Place:
    def __init__(self):
        self.frame, self.space = lax.axis_index("frame"), lax.axis_index("space")
        self.base = self.space // 2 * 2
        self.z = self.space // 2
        self.lo = self.space % 2
        self.y = self.frame // 8 * 2 + self.lo
        self.x = self.frame // 2 % 4
        self.core = self.frame % 2
        self.turn = self.turn_of(self.x, self.y, self.core)
        self.slot = self.slot_of(self.y, self.frame)
        self.start = self.start_of(self.y, self.turn)

    def turn_of(self, x, y, core):
        return (x + y) % 4 * 2 + core

    def start_of(self, y, turn):
        return 25 * y + 3 * turn

    def slot_of(self, y, frame):
        return y % 2 * HALF + frame

    def frame_of(self, x, y, core):
        return y // 2 * 8 + x * 2 + core

    def device(self, y, frame):
        return (frame, self.base + y % 2)


FAR_X = (2, 1, 3, 0)


def for_peers(place, body, each_y=None):
    def one_y(y, skip_self):
        for dx in FAR_X:
            for dc in (1, 0):
                if skip_self and dx == 0 and dc == 0:
                    continue
                x, core = (place.x + dx) % 4, (place.core + dc) % 2
                body(y, place.turn_of(x, y, core), place.frame_of(x, y, core))

    @pl.loop(0, 7)
    def _(a):
        dy = (1 - a % 2) * (4 + a // 2) + a % 2 * (4 - (a + 1) // 2)
        y = (place.y + dy) % 8
        one_y(y, False)
        if each_y is not None:
            each_y(y)

    one_y(place.y, True)
    if each_y is not None:

        @pl.when(place.turn != 7)
        def _():
            each_y(place.y)


def by_turn(place, body):
    @pl.when(place.turn != 7)
    def _():
        body(3)

    @pl.when(place.turn == 7)
    def _():
        body(4)


def wait_bytes(ref, semaphore):
    pltpu.make_async_copy(ref, ref, semaphore).wait()


def kernel(
    image, maps, measured, lines, weights, noise, row_table, time_table,
    out,
    send, ret, recv, back, below, above, planes, noise_planes, raw_maps, coil_planes, lines_planes,
    line_buf, weight_buf, row_buf, time_buf, spectra, moved, total, result,
    load_sem, own_sem, fwd_send, fwd_recv, ret_send, ret_recv, z_send, z_recv,
):
    place = Place()
    loads = [
        [pltpu.make_async_copy(image.at[f, 0, :, i, :], planes.at[f, i], load_sem.at[0]) for f in range(2) for i in range(2)],
        [pltpu.make_async_copy(image.at[f, 0, :, :, pl.ds(0, MAIN)], send.at[pl.ds(0, ROWS), f], load_sem.at[1]) for f in range(2)],
        [pltpu.make_async_copy(maps.at[0], raw_maps, load_sem.at[2])],
        [
            pltpu.make_async_copy(row_table, row_buf, load_sem.at[3]),
            pltpu.make_async_copy(lines, line_buf, load_sem.at[3]),
            pltpu.make_async_copy(weights, weight_buf, load_sem.at[3]),
            pltpu.make_async_copy(time_table, time_buf, load_sem.at[3]),
        ],
        [pltpu.make_async_copy(measured.at[f, 0, :, :, i, :], lines_planes.at[f, :, i], load_sem.at[4]) for f in range(2) for i in range(2)],
        [pltpu.make_async_copy(noise.at[f, 0, :, i, :], noise_planes.at[f, i], load_sem.at[5]) for f in range(2) for i in range(2)],
    ]
    for group in loads:
        for copy in group:
            copy.start()

    def finish(which):
        for copy in loads[which]:
            copy.wait()

    barrier = pltpu.get_barrier_semaphore()

    def greet(y, turn, frame):
        pl.semaphore_signal(barrier, inc=1, device_id=place.device(y, frame), device_id_type=MESH)

    for_peers(place, greet)

    @pl.when(place.z < 7)
    def _():
        pl.semaphore_signal(barrier, inc=1, device_id=(place.frame, place.space + 2), device_id_type=MESH)

    @pl.when(place.z > 0)
    def _():
        pl.semaphore_signal(barrier, inc=1, device_id=(place.frame, place.space - 2), device_id_type=MESH)

    finish(0)
    finish(1)
    for f in range(2):
        for i in range(2):
            tails = [planes[f, i, 40 * b : 40 * b + 40, MAIN:COLS] for b in range(4)]
            send[pl.ds(ROWS, 40), f, i, :] = jnp.concatenate(tails, axis=1)

    finish(2)

    @pl.loop(0, COILS)
    def _(c):
        for i in range(2):
            coil_planes[c, i] = raw_maps[c, :, i, :].astype(F32)

    @pl.when((place.z == 0) | (place.z == 7))
    def _():
        pl.semaphore_wait(barrier, PEERS)

    @pl.when((place.z != 0) & (place.z != 7))
    def _():
        pl.semaphore_wait(barrier, PEERS + 1)

    def send_fwd(y, turn, frame):
        pltpu.make_async_remote_copy(
            send.at[pl.ds(place.start_of(y, turn), 3)],
            recv.at[pl.ds(0, 3), place.slot],
            fwd_send, fwd_recv, device_id=place.device(y, frame), device_id_type=MESH,
        ).start()

    def send_extra(y):
        frame = place.frame_of((7 - y) % 4, y, 1)
        pltpu.make_async_remote_copy(
            send.at[pl.ds(25 * y + 24, 1)],
            recv.at[pl.ds(3, 1), place.slot],
            fwd_send, fwd_recv, device_id=place.device(y, frame), device_id_type=MESH,
        ).start()

    for_peers(place, send_fwd, send_extra)

    def keep_own(count):
        copy = pltpu.make_async_copy(send.at[pl.ds(place.start, count)], recv.at[pl.ds(0, count), place.slot], own_sem)
        copy.start()
        copy.wait()

    by_turn(place, keep_own)

    finish(3)
    finish(4)
    real, imag = row_buf[0], row_buf[1]
    positions = lax.broadcasted_iota(jnp.int32, (COLS, LINES), 0)

    @pl.loop(0, 2)
    def _(f):
        chosen = (positions == line_buf[pl.ds(f, 1), :]).astype(F32).astype(BF16)
        pick = (((0,), (0,)), ((), ()))
        line_real = lax.dot_general(chosen, real, pick, preferred_element_type=F32)
        line_imag = lax.dot_general(chosen, imag, pick, preferred_element_type=F32)
        table = jnp.concatenate([line_real, line_imag], axis=0)
        turned = jnp.concatenate([-line_imag, line_real], axis=0)
        back_table = jnp.concatenate([table.T, turned.T], axis=0).astype(BF16)
        table = table.astype(BF16)
        x_re, x_im = planes[f, 0], planes[f, 1]

        @pl.loop(0, COILS, unroll=2)
        def _(c):
            s_re, s_im = coil_planes[c, 0], coil_planes[c, 1]
            c_re = (s_re * x_re - s_im * x_im).astype(BF16)
            c_im = (s_re * x_im + s_im * x_re).astype(BF16)
            first, second = dot(table, c_re), dot(table, c_im)
            spectra[c, 0:LINES] = first[:LINES] - second[LINES:]
            spectra[c, LINES:] = first[LINES:] + second[:LINES]

        @pl.loop(0, COILS, unroll=2)
        def _(c):
            rows = spectra[c].astype(BF16)
            first, second = dot(rows, real), dot(rows, imag)
            res_re = first[:LINES] - second[LINES:] - lines_planes[f, c, 0]
            res_im = first[LINES:] + second[:LINES] - lines_planes[f, c, 1]
            residual = jnp.concatenate([res_re, res_im], axis=0).astype(BF16)
            first, second = dot(residual, real), dot(residual, imag)
            moved[c, 0:LINES] = first[:LINES] + second[LINES:]
            moved[c, LINES:] = first[LINES:] - second[:LINES]

        total[...] = jnp.zeros_like(total)

        @pl.loop(0, COILS, unroll=2)
        def _(c):
            full = dot(back_table, moved[c].astype(BF16))
            s_re, s_im = coil_planes[c, 0], coil_planes[c, 1]
            b_re, b_im = full[:ROWS], full[ROWS:]
            total[0] += s_re * b_re + s_im * b_im
            total[1] += s_re * b_im - s_im * b_re

        for i in range(2):
            result[f, i] = 0.75 * planes[f, i] - 0.5 * total[i]

    finish(5)
    for f in range(2):
        for i in range(2):
            result[f, i] += noise_planes[f, i]

    spot = (lax.broadcasted_iota(jnp.int32, (FRAMES, FRAMES), 0) == lax.broadcasted_iota(jnp.int32, (FRAMES, FRAMES), 1))
    column = -0.5 * jnp.sum(jnp.where(spot, weight_buf[...], 0.0), axis=1, keepdims=True)

    def up_copy(count):
        return pltpu.make_async_remote_copy(
            recv.at[pl.ds(0, count), pl.ds(HALF, HALF)], below.at[pl.ds(0, count)],
            z_send.at[0], z_recv.at[0], device_id=(place.frame, place.space + 2), device_id_type=MESH,
        )

    def down_copy(count):
        return pltpu.make_async_remote_copy(
            recv.at[pl.ds(0, count), pl.ds(0, HALF)], above.at[pl.ds(0, count)],
            z_send.at[1], z_recv.at[1], device_id=(place.frame, place.space - 2), device_id_type=MESH,
        )

    def prior(count):
        wait_bytes(recv.at[pl.ds(0, count), pl.ds(0, PEERS - 1)], fwd_recv)

        @pl.when(place.z < 7)
        def _():
            up_copy(count).start()

        @pl.when(place.z > 0)
        def _():
            down_copy(count).start()

        rows_in, rows_out = recv.reshape(4 * 4 * PEERS, MAIN), back.reshape(4 * 4 * PEERS, MAIN)
        rows_below, rows_above = below.reshape(4 * 4 * HALF, MAIN), above.reshape(4 * 4 * HALF, MAIN)

        def span(first, g):
            return pl.ds(4 * (PEERS * g + first), 4 * HALF)

        blocks = [(first, g) for first in (0, HALF) for g in range(count)]
        stack = jnp.concatenate([rows_in[span(first, g), :] for first, g in blocks], axis=1)
        spectrum = exact_dot(time_buf[0], stack)
        s_re, s_im = spectrum[:FRAMES], spectrum[FRAMES:]
        scale = column * lax.rsqrt(s_re * s_re + s_im * s_im + SOFTNESS)
        shrunk = jnp.concatenate([s_re * scale, s_im * scale], axis=0)
        gradient = exact_dot(time_buf[1], shrunk)
        for n, (first, g) in enumerate(blocks):
            beside = rows_in[span(HALF - first, g), :]
            rows_out[span(first, g), :] = gradient[:, n * MAIN : (n + 1) * MAIN] + 0.125 * beside

        @pl.when(place.z > 0)
        def _():
            up_copy(count).wait_recv()
            for g in range(count):
                rows_out[span(0, g), :] += 0.125 * rows_below[pl.ds(4 * HALF * g, 4 * HALF), :]

        @pl.when(place.z < 7)
        def _():
            down_copy(count).wait_recv()
            for g in range(count):
                rows_out[span(HALF, g), :] += 0.125 * rows_above[pl.ds(4 * HALF * g, 4 * HALF), :]

        def send_back(y, turn, frame):
            pltpu.make_async_remote_copy(
                back.at[pl.ds(0, count), place.slot_of(y, frame)],
                ret.at[pl.ds(place.start, count)],
                ret_send, ret_recv, device_id=place.device(y, frame), device_id_type=MESH,
            ).start()

        for_peers(place, send_back)
        copy = pltpu.make_async_copy(back.at[pl.ds(0, count), place.slot], ret.at[pl.ds(place.start, count)], own_sem)
        copy.start()
        copy.wait()
        wait_bytes(ret.at[pl.ds(0, GROUPS - count)], ret_recv)

    by_turn(place, prior)

    for f in range(2):
        for i in range(2):
            out[f, 0, :, i, 0:MAIN] = result[f, i, :, 0:MAIN] + ret[pl.ds(0, ROWS), f, i, :]
            tails = ret[pl.ds(ROWS, 40), f, i, :]
            tails = jnp.concatenate([tails[:, 32 * b : 32 * b + 32] for b in range(4)], axis=0)
            out[f, 0, :, i, MAIN:COLS] = result[f, i, :, MAIN:COLS] + tails

    def drain(count):
        wait_bytes(send.at[pl.ds(0, GROUPS - count)], fwd_send)
        wait_bytes(recv.at[pl.ds(0, count), pl.ds(0, PEERS - 1)], ret_send)

        @pl.when(place.z < 7)
        def _():
            up_copy(count).wait_send()

        @pl.when(place.z > 0)
        def _():
            down_copy(count).wait_send()

    by_turn(place, drain)


def on_device(image, maps, measured, lines, weights, noise):
    dma = pltpu.SemaphoreType.DMA
    anywhere = pl.BlockSpec(memory_space=pl.ANY)
    return pl.pallas_call(
        kernel,
        name="langevin_step",
        out_shape=jax.ShapeDtypeStruct(image.shape, F32),
        in_specs=[anywhere] * 8,
        out_specs=pl.BlockSpec(memory_space=pltpu.VMEM),
        scratch_shapes=[
            pltpu.VMEM((GROUPS, 2, 2, MAIN), F32),
            pltpu.VMEM((GROUPS, 2, 2, MAIN), F32),
            pltpu.VMEM((4, PEERS, 2, 2, MAIN), F32),
            pltpu.VMEM((4, PEERS, 2, 2, MAIN), F32),
            pltpu.VMEM((4, HALF, 2, 2, MAIN), F32),
            pltpu.VMEM((4, HALF, 2, 2, MAIN), F32),
            pltpu.VMEM((2, 2, ROWS, COLS), F32),
            pltpu.VMEM((2, 2, ROWS, COLS), F32),
            pltpu.VMEM((COILS, ROWS, 2, COLS), BF16),
            pltpu.VMEM((COILS, 2, ROWS, COLS), F32),
            pltpu.VMEM((2, COILS, 2, LINES, COLS), F32),
            pltpu.VMEM((2, LINES), jnp.int32),
            pltpu.VMEM((1, FRAMES), F32),
            pltpu.VMEM((2, COLS, COLS), BF16),
            pltpu.VMEM((2, 2 * FRAMES, 2 * FRAMES), F32),
            pltpu.VMEM((COILS, 2 * LINES, COLS), F32),
            pltpu.VMEM((COILS, 2 * LINES, COLS), F32),
            pltpu.VMEM((2, ROWS, COLS), F32),
            pltpu.VMEM((2, 2, ROWS, COLS), F32),
            dma((6,)), dma, dma, dma, dma, dma, dma((2,)), dma((2,)),
        ],
        compiler_params=pltpu.CompilerParams(collective_id=0, has_side_effects=True, vmem_limit_bytes=40 << 20),
        cost_estimate=pl.CostEstimate(flops=2_000_000_000, bytes_accessed=6_000_000, transcendentals=60_000),
    )(image, maps, measured, lines, weights.reshape(1, FRAMES), noise, jnp.asarray(row_tables()), jnp.asarray(time_tables()))


def solution(mesh):
    return jax.shard_map(
        on_device,
        mesh=mesh,
        in_specs=(
            P("frame", "space", None, None, None),
            P("space", None, None, None, None),
            P("frame", "space", None, None, None, None),
            P("frame", None),
            P(),
            P("frame", "space", None, None, None),
        ),
        out_specs=P("frame", "space", None, None, None),
        check_vma=False,
    )
```

time: 110 us -> 53.3 us (0.48)
  the two profiles are of different devices: /device:TPU:201 before, /device:TPU:1 now
where the time goes in v1:
time: 53.3 us; the launch traced here: 52.6 us
  Pallas kernels  43.8 us (82%)
  local copies, waits for them, and re-layouts  8.8 us (17%)
    pallas_call x1, Pallas kernels, on_device(): pl.pallas_call(kernel, name='langevin_step', out_shape=jax.ShapeDtypeStru...  43.8 us
    unnamed x17, local copies, waits for them, and re-layouts  8.8 us

profile of v1, /device:TPU:1, one launch (start us, length us, event | category | flops | bytes accessed | tf_op | source)
XLA Modules:
  0.0 52.6 jit_solution(4005813311990029297)
XLA Ops:
  0.0 0.0 copy-start
  0.0 1.3 %copy-done = bf16[1,8,160,2,160]{4,3,2,1,0:T(2,128)(2,1)S(1)} copy-done((bf16[1,8,160,2,160]{4,3,2,1,0:T(2,128)(2,1)S(1)}, bf16[1,8,160,2,160]{4,3,2,1,0:T(2,128)(2,1)}, u32[]{:S(2)}) %copy-start) | copy-done | bytes 819224
  1.3 0.0 copy-start.1
  1.3 1.3 %copy-done.1 = f32[2,1,8,40,2,160]{5,4,3,2,1,0:T(2,128)S(1)} copy-done((f32[2,1,8,40,2,160]{5,4,3,2,1,0:T(2,128)S(1)}, f32[2,1,8,40,2,160]{5,4,3,2,1,0:T(2,128)}, u32[]{:S(2)}) %copy-start.1) | copy-done | bytes 819224
  2.6 0.0 copy-start.2
  2.6 1.1 %copy-done.2 = f32[2,1,160,2,160]{4,3,2,1,0:T(2,128)S(1)} copy-done((f32[2,1,160,2,160]{4,3,2,1,0:T(2,128)S(1)}, f32[2,1,160,2,160]{4,3,2,1,0:T(2,128)}, u32[]{:S(2)}) %copy-start.2) | copy-done | bytes 409624
  3.7 0.0 copy-start.3
  3.7 1.1 %copy-done.3 = f32[2,1,160,2,160]{4,3,2,1,0:T(2,128)S(1)} copy-done((f32[2,1,160,2,160]{4,3,2,1,0:T(2,128)S(1)}, f32[2,1,160,2,160]{4,3,2,1,0:T(2,128)}, u32[]{:S(2)}) %copy-start.3) | copy-done | bytes 409624
  4.8 0.0 copy-start.4
  4.8 0.7 %copy-done.4 = s32[2,40]{1,0:T(2,128)S(1)} copy-done((s32[2,40]{1,0:T(2,128)S(1)}, s32[2,40]{1,0:T(2,128)}, u32[]{:S(2)}) %copy-start.4) | copy-done | bytes 344
  5.5 0.0 copy-start.5
  5.5 0.7 %copy-done.5 = f32[64]{0:T(128)S(1)} copy-done((f32[64]{0:T(128)S(1)}, f32[64]{0:T(128)}, u32[]{:S(2)}) %copy-start.5) | copy-done | bytes 280
  6.1 0.0 copy-start.6
  6.1 0.9 %copy-done.6 = bf16[2,160,160]{2,1,0:T(8,128)(2,1)S(1)} copy-done((bf16[2,160,160]{2,1,0:T(8,128)(2,1)S(1)}, bf16[2,160,160]{2,1,0:T(8,128)(2,1)}, u32[]{:S(2)}) %copy-start.6) | copy-done | bytes 102424
  7.1 0.0 copy-start.7
  7.1 0.9 %copy-done.7 = f32[2,128,128]{2,1,0:T(8,128)S(1)} copy-done((f32[2,128,128]{2,1,0:T(8,128)S(1)}, f32[2,128,128]{2,1,0:T(8,128)}, u32[]{:S(2)}) %copy-start.7) | copy-done | bytes 131096
  8.0 43.8 %langevin_step.1 = f32[2,1,160,2,160]{4,3,2,1,0:T(2,128)S(1)} custom-call(f32[2,1,160,2,160]{4,3,2,1,0:T(2,128)S(1)} %copy-done.2, bf16[1,8,160,2,160]{4,3,2,1,0:T(2,128)(2,1)S(1)} %copy-done, f32[2,1,8,40,2,160]{5,4,3,2,1,0:T(2,128)S(1)} %copy-done.1, s32[2,40]{1,0:T(2,128)S(1)} %copy-done.4, f32[1,64]{1,0:T(1,128)S(1)} %bitcast.1, ...), custom_call_target="tpu_custom_call" | custom-call | flops 2000000000 | bytes 6000000 | tf_op jit(solution)/shard_map/langevin_step/pallas_call | solution.py:361
  51.7 0.8 %copy.10 = f32[2,1,160,2,160]{4,3,2,1,0:T(2,128)} copy(f32[2,1,160,2,160]{4,3,2,1,0:T(2,128)S(1)} %langevin_step.1) | data formatting | bytes 819200
Async XLA Ops:
  0.0 1.3 %copy-start = (bf16[1,8,160,2,160]{4,3,2,1,0:T(2,128)(2,1)S(1)}, bf16[1,8,160,2,160]{4,3,2,1,0:T(2,128)(2,1)}, u32[]{:S(2)}) copy-start(bf16[1,8,160,2,160]{4,3,2,1,0:T(2,128)(2,1)} %maps.1) | copy-start | bytes 2457604
  1.3 1.3 %copy-start.1 = (f32[2,1,8,40,2,160]{5,4,3,2,1,0:T(2,128)S(1)}, f32[2,1,8,40,2,160]{5,4,3,2,1,0:T(2,128)}, u32[]{:S(2)}) copy-start(f32[2,1,8,40,2,160]{5,4,3,2,1,0:T(2,128)} %measured.1) | copy-start | bytes 2457604
  2.6 1.1 %copy-start.2 = (f32[2,1,160,2,160]{4,3,2,1,0:T(2,128)S(1)}, f32[2,1,160,2,160]{4,3,2,1,0:T(2,128)}, u32[]{:S(2)}) copy-start(f32[2,1,160,2,160]{4,3,2,1,0:T(2,128)} %image.1) | copy-start | bytes 1228804
  3.7 1.1 %copy-start.3 = (f32[2,1,160,2,160]{4,3,2,1,0:T(2,128)S(1)}, f32[2,1,160,2,160]{4,3,2,1,0:T(2,128)}, u32[]{:S(2)}) copy-start(f32[2,1,160,2,160]{4,3,2,1,0:T(2,128)} %noise.1) | copy-start | bytes 1228804
  4.8 0.7 %copy-start.4 = (s32[2,40]{1,0:T(2,128)S(1)}, s32[2,40]{1,0:T(2,128)}, u32[]{:S(2)}) copy-start(s32[2,40]{1,0:T(2,128)} %lines.1) | copy-start | bytes 964
  5.5 0.7 %copy-start.5 = (f32[64]{0:T(128)S(1)}, f32[64]{0:T(128)}, u32[]{:S(2)}) copy-start(f32[64]{0:T(128)} %param.12) | copy-start | bytes 772
  6.1 0.9 %copy-start.6 = (bf16[2,160,160]{2,1,0:T(8,128)(2,1)S(1)}, bf16[2,160,160]{2,1,0:T(8,128)(2,1)}, u32[]{:S(2)}) copy-start(bf16[2,160,160]{2,1,0:T(8,128)(2,1)} %constant.4.clone.row_table) | copy-start | bytes 307204
  7.1 0.9 %copy-start.7 = (f32[2,128,128]{2,1,0:T(8,128)S(1)}, f32[2,128,128]{2,1,0:T(8,128)}, u32[]{:S(2)}) copy-start(f32[2,128,128]{2,1,0:T(8,128)} %constant.5.clone.time_table) | copy-start | bytes 393220

commit v2 on v1

--- a/solution.py
+++ b/solution.py
@@ -122,7 +122,7 @@
     image, maps, measured, lines, weights, noise, row_table, time_table,
     out,
     send, ret, recv, back, below, above, planes, noise_planes, raw_maps, coil_planes, lines_planes,
-    line_buf, weight_buf, row_buf, time_buf, spectra, moved, total, result,
+    line_buf, weight_buf, row_buf, time_buf, back_table, spectra, moved, total, result,
     load_sem, own_sem, fwd_send, fwd_recv, ret_send, ret_recv, z_send, z_recv,
 ):
     place = Place()
@@ -184,22 +184,24 @@
     def _():
         pl.semaphore_wait(barrier, PEERS + 1)
 
-    def send_fwd(y, turn, frame):
-        pltpu.make_async_remote_copy(
-            send.at[pl.ds(place.start_of(y, turn), 3)],
-            recv.at[pl.ds(0, 3), place.slot],
-            fwd_send, fwd_recv, device_id=place.device(y, frame), device_id_type=MESH,
-        ).start()
-
-    def send_extra(y):
-        frame = place.frame_of((7 - y) % 4, y, 1)
-        pltpu.make_async_remote_copy(
-            send.at[pl.ds(25 * y + 24, 1)],
-            recv.at[pl.ds(3, 1), place.slot],
-            fwd_send, fwd_recv, device_id=place.device(y, frame), device_id_type=MESH,
-        ).start()
-
-    for_peers(place, send_fwd, send_extra)
+    for k in range(3):
+
+        def send_fwd(y, turn, frame):
+            pltpu.make_async_remote_copy(
+                send.at[pl.ds(place.start_of(y, turn) + k, 1)],
+                recv.at[pl.ds(k, 1), place.slot],
+                fwd_send, fwd_recv.at[k], device_id=place.device(y, frame), device_id_type=MESH,
+            ).start()
+
+        def send_extra(y):
+            frame = place.frame_of((7 - y) % 4, y, 1)
+            pltpu.make_async_remote_copy(
+                send.at[pl.ds(25 * y + 24, 1)],
+                recv.at[pl.ds(3, 1), place.slot],
+                fwd_send, fwd_recv.at[2], device_id=place.device(y, frame), device_id_type=MESH,
+            ).start()
+
+        for_peers(place, send_fwd, send_extra if k == 2 else None)
 
     def keep_own(count):
         copy = pltpu.make_async_copy(send.at[pl.ds(place.start, count)], recv.at[pl.ds(0, count), place.slot], own_sem)
@@ -210,18 +212,18 @@
 
     finish(3)
     finish(4)
+    finish(5)
     real, imag = row_buf[0], row_buf[1]
     positions = lax.broadcasted_iota(jnp.int32, (COLS, LINES), 0)
 
-    @pl.loop(0, 2)
-    def _(f):
+    def to_lines(f):
         chosen = (positions == line_buf[pl.ds(f, 1), :]).astype(F32).astype(BF16)
         pick = (((0,), (0,)), ((), ()))
         line_real = lax.dot_general(chosen, real, pick, preferred_element_type=F32)
         line_imag = lax.dot_general(chosen, imag, pick, preferred_element_type=F32)
         table = jnp.concatenate([line_real, line_imag], axis=0)
         turned = jnp.concatenate([-line_imag, line_real], axis=0)
-        back_table = jnp.concatenate([table.T, turned.T], axis=0).astype(BF16)
+        back_table[...] = jnp.concatenate([table.T, turned.T], axis=0).astype(BF16)
         table = table.astype(BF16)
         x_re, x_im = planes[f, 0], planes[f, 1]
 
@@ -234,6 +236,7 @@
             spectra[c, 0:LINES] = first[:LINES] - second[LINES:]
             spectra[c, LINES:] = first[LINES:] + second[:LINES]
 
+    def to_residual(f):
         @pl.loop(0, COILS, unroll=2)
         def _(c):
             rows = spectra[c].astype(BF16)
@@ -245,57 +248,53 @@
             moved[c, 0:LINES] = first[:LINES] + second[LINES:]
             moved[c, LINES:] = first[LINES:] - second[:LINES]
 
+    def to_image(f):
         total[...] = jnp.zeros_like(total)
 
         @pl.loop(0, COILS, unroll=2)
         def _(c):
-            full = dot(back_table, moved[c].astype(BF16))
+            full = dot(back_table[...], moved[c].astype(BF16))
             s_re, s_im = coil_planes[c, 0], coil_planes[c, 1]
             b_re, b_im = full[:ROWS], full[ROWS:]
             total[0] += s_re * b_re + s_im * b_im
             total[1] += s_re * b_im - s_im * b_re
 
         for i in range(2):
-            result[f, i] = 0.75 * planes[f, i] - 0.5 * total[i]
-
-    finish(5)
-    for f in range(2):
-        for i in range(2):
-            result[f, i] += noise_planes[f, i]
+            result[f, i] = 0.75 * planes[f, i] - 0.5 * total[i] + noise_planes[f, i]
 
     spot = (lax.broadcasted_iota(jnp.int32, (FRAMES, FRAMES), 0) == lax.broadcasted_iota(jnp.int32, (FRAMES, FRAMES), 1))
     column = -0.5 * jnp.sum(jnp.where(spot, weight_buf[...], 0.0), axis=1, keepdims=True)
 
-    def up_copy(count):
+    def up_copy(k, count):
         return pltpu.make_async_remote_copy(
-            recv.at[pl.ds(0, count), pl.ds(HALF, HALF)], below.at[pl.ds(0, count)],
-            z_send.at[0], z_recv.at[0], device_id=(place.frame, place.space + 2), device_id_type=MESH,
+            recv.at[pl.ds(k, count), pl.ds(HALF, HALF)], below.at[pl.ds(k, count)],
+            z_send.at[k, 0], z_recv.at[k, 0], device_id=(place.frame, place.space + 2), device_id_type=MESH,
         )
 
-    def down_copy(count):
+    def down_copy(k, count):
         return pltpu.make_async_remote_copy(
-            recv.at[pl.ds(0, count), pl.ds(0, HALF)], above.at[pl.ds(0, count)],
-            z_send.at[1], z_recv.at[1], device_id=(place.frame, place.space - 2), device_id_type=MESH,
+            recv.at[pl.ds(k, count), pl.ds(0, HALF)], above.at[pl.ds(k, count)],
+            z_send.at[k, 1], z_recv.at[k, 1], device_id=(place.frame, place.space - 2), device_id_type=MESH,
         )
 
-    def prior(count):
-        wait_bytes(recv.at[pl.ds(0, count), pl.ds(0, PEERS - 1)], fwd_recv)
+    rows_in, rows_out = recv.reshape(4 * 4 * PEERS, MAIN), back.reshape(4 * 4 * PEERS, MAIN)
+    rows_below, rows_above = below.reshape(4 * 4 * HALF, MAIN), above.reshape(4 * 4 * HALF, MAIN)
+
+    def span(first, g):
+        return pl.ds(4 * (PEERS * g + first), 4 * HALF)
+
+    def arrive(k, count):
+        wait_bytes(recv.at[pl.ds(k, count), pl.ds(0, PEERS - 1)], fwd_recv.at[k])
 
         @pl.when(place.z < 7)
         def _():
-            up_copy(count).start()
+            up_copy(k, count).start()
 
         @pl.when(place.z > 0)
         def _():
-            down_copy(count).start()
-
-        rows_in, rows_out = recv.reshape(4 * 4 * PEERS, MAIN), back.reshape(4 * 4 * PEERS, MAIN)
-        rows_below, rows_above = below.reshape(4 * 4 * HALF, MAIN), above.reshape(4 * 4 * HALF, MAIN)
-
-        def span(first, g):
-            return pl.ds(4 * (PEERS * g + first), 4 * HALF)
-
-        blocks = [(first, g) for first in (0, HALF) for g in range(count)]
+            down_copy(k, count).start()
+
+        blocks = [(first, g) for first in (0, HALF) for g in range(k, k + count)]
         stack = jnp.concatenate([rows_in[span(first, g), :] for first, g in blocks], axis=1)
         spectrum = exact_dot(time_buf[0], stack)
         s_re, s_im = spectrum[:FRAMES], spectrum[FRAMES:]
@@ -306,32 +305,48 @@
             beside = rows_in[span(HALF - first, g), :]
             rows_out[span(first, g), :] = gradient[:, n * MAIN : (n + 1) * MAIN] + 0.125 * beside
 
+    def leave(k, count):
         @pl.when(place.z > 0)
         def _():
-            up_copy(count).wait_recv()
-            for g in range(count):
+            up_copy(k, count).wait_recv()
+            for g in range(k, k + count):
                 rows_out[span(0, g), :] += 0.125 * rows_below[pl.ds(4 * HALF * g, 4 * HALF), :]
 
         @pl.when(place.z < 7)
         def _():
-            down_copy(count).wait_recv()
-            for g in range(count):
+            down_copy(k, count).wait_recv()
+            for g in range(k, k + count):
                 rows_out[span(HALF, g), :] += 0.125 * rows_above[pl.ds(4 * HALF * g, 4 * HALF), :]
 
         def send_back(y, turn, frame):
             pltpu.make_async_remote_copy(
-                back.at[pl.ds(0, count), place.slot_of(y, frame)],
-                ret.at[pl.ds(place.start, count)],
+                back.at[pl.ds(k, count), place.slot_of(y, frame)],
+                ret.at[pl.ds(place.start + k, count)],
                 ret_send, ret_recv, device_id=place.device(y, frame), device_id_type=MESH,
             ).start()
 
         for_peers(place, send_back)
+
+    to_lines(0)
+    arrive(0, 1)
+    to_residual(0)
+    arrive(1, 1)
+    leave(0, 1)
+    by_turn(place, lambda count: arrive(2, count - 2))
+    leave(1, 1)
+    to_image(0)
+    by_turn(place, lambda count: leave(2, count - 2))
+    to_lines(1)
+    to_residual(1)
+    to_image(1)
+
+    def settle(count):
         copy = pltpu.make_async_copy(back.at[pl.ds(0, count), place.slot], ret.at[pl.ds(place.start, count)], own_sem)
         copy.start()
         copy.wait()
         wait_bytes(ret.at[pl.ds(0, GROUPS - count)], ret_recv)
 
-    by_turn(place, prior)
+    by_turn(place, settle)
 
     for f in range(2):
         for i in range(2):
@@ -344,13 +359,16 @@
         wait_bytes(send.at[pl.ds(0, GROUPS - count)], fwd_send)
         wait_bytes(recv.at[pl.ds(0, count), pl.ds(0, PEERS - 1)], ret_send)
 
-        @pl.when(place.z < 7)
-        def _():
-            up_copy(count).wait_send()
-
-        @pl.when(place.z > 0)
-        def _():
-            down_copy(count).wait_send()
+        for k in range(3):
+            groups = count - 2 if k == 2 else 1
+
+            @pl.when(place.z < 7)
+            def _():
+                up_copy(k, groups).wait_send()
+
+            @pl.when(place.z > 0)
+            def _():
+                down_copy(k, groups).wait_send()
 
     by_turn(place, drain)
 
@@ -380,13 +398,14 @@
             pltpu.VMEM((1, FRAMES), F32),
             pltpu.VMEM((2, COLS, COLS), BF16),
             pltpu.VMEM((2, 2 * FRAMES, 2 * FRAMES), F32),
+            pltpu.VMEM((2 * ROWS, 2 * LINES), BF16),
             pltpu.VMEM((COILS, 2 * LINES, COLS), F32),
             pltpu.VMEM((COILS, 2 * LINES, COLS), F32),
             pltpu.VMEM((2, ROWS, COLS), F32),
             pltpu.VMEM((2, 2, ROWS, COLS), F32),
-            dma((6,)), dma, dma, dma, dma, dma, dma((2,)), dma((2,)),
+            dma((6,)), dma, dma, dma((3,)), dma, dma, dma((3, 2)), dma((3, 2)),
         ],
-        compiler_params=pltpu.CompilerParams(collective_id=0, has_side_effects=True, vmem_limit_bytes=40 << 20),
+        compiler_params=pltpu.CompilerParams(collective_id=0, has_side_effects=True, vmem_limit_bytes=60 << 20),
         cost_estimate=pl.CostEstimate(flops=2_000_000_000, bytes_accessed=6_000_000, transcendentals=60_000),
     )(image, maps, measured, lines, weights.reshape(1, FRAMES), noise, jnp.asarray(row_tables()), jnp.asarray(time_tables()))
 

time: 53.3 us -> 37.8 us (0.71); the launches traced: 52.6 us -> 37.7 us
  Pallas kernels: 43.8 us -> 35.5 us
  local copies, waits for them, and re-layouts: 8.8 us -> 2.15 us
    pallas_call x1, Pallas kernels: 43.8 us -> 35.5 us  [on_device(): pl.pallas_call(kernel, name='langevin_step', out_shape=jax.ShapeDtypeStru...]
    unnamed x17 -> x1, local copies, waits for them, and re-layouts: 8.8 us -> 2.15 us
where the time goes in v2:
time: 37.8 us; the launch traced here: 37.7 us
  Pallas kernels  35.5 us (94%)
  local copies, waits for them, and re-layouts  2.15 us (6%)
    pallas_call x1, Pallas kernels, on_device(): pl.pallas_call(kernel, name='langevin_step', out_shape=jax.ShapeDtypeStru...  35.5 us
    unnamed x1, local copies, waits for them, and re-layouts  2.15 us

profile of v2, /device:TPU:1, one launch (start us, length us, event | category | flops | bytes accessed | tf_op | source)
XLA Modules:
  0.0 37.7 jit_solution(6648567088655224581)
XLA Ops:
  0.0 35.5 %langevin_step.1 = f32[2,1,160,2,160]{4,3,2,1,0:T(2,128)} custom-call(f32[2,1,160,2,160]{4,3,2,1,0:T(2,128)} %image.1, bf16[1,8,160,2,160]{4,3,2,1,0:T(2,128)(2,1)} %maps.1, f32[2,1,8,40,2,160]{5,4,3,2,1,0:T(2,128)} %measured.1, s32[2,40]{1,0:T(2,128)} %lines.1, f32[1,64]{1,0:T(1,128)} %bitcast.1, f32[2,1,160,2,160]{4,3,2,1,0:T(2,128)} %noise.1, ...), custom_call_target="tpu_custom_call" | custom-call | flops 2000000000 | bytes 6000000 | tf_op jit(solution)/shard_map/langevin_step/pallas_call | solution.py:379
  35.5 2.1 %copy.10 = f32[2,1,160,2,160]{4,3,2,1,0:T(2,128)} copy(f32[2,1,160,2,160]{4,3,2,1,0:T(2,128)} %langevin_step.1) | data formatting | bytes 819200

commit v3 on v2

--- a/solution.py
+++ b/solution.py
@@ -52,56 +52,53 @@
         self.frame, self.space = lax.axis_index("frame"), lax.axis_index("space")
         self.base = self.space // 2 * 2
         self.z = self.space // 2
-        self.lo = self.space % 2
-        self.y = self.frame // 8 * 2 + self.lo
-        self.x = self.frame // 2 % 4
-        self.core = self.frame % 2
-        self.turn = self.turn_of(self.x, self.y, self.core)
-        self.slot = self.slot_of(self.y, self.frame)
-        self.start = self.start_of(self.y, self.turn)
-
-    def turn_of(self, x, y, core):
-        return (x + y) % 4 * 2 + core
-
-    def start_of(self, y, turn):
-        return 25 * y + 3 * turn
-
-    def slot_of(self, y, frame):
-        return y % 2 * HALF + frame
-
-    def frame_of(self, x, y, core):
-        return y // 2 * 8 + x * 2 + core
-
-    def device(self, y, frame):
-        return (frame, self.base + y % 2)
+        self.y = self.frame // 8 * 2 + self.space % 2
+        x, core = self.frame // 2 % 4, self.frame % 2
+        self.xs = [(x + dx) % 4 for dx in FAR_X]
+        self.cores = [1 - core, core]
+        self.turn = (x + self.y) % 4 * 2 + core
+        self.slot = self.space % 2 * HALF + self.frame
+        self.start = 25 * self.y + 3 * self.turn
+
+
+class Peer:
+    def __init__(self, frame, space, slot, start):
+        self.device, self.slot, self.start = (frame, space), slot, start
 
 
 FAR_X = (2, 1, 3, 0)
 
 
-def for_peers(place, body, each_y=None):
-    def one_y(y, skip_self):
-        for dx in FAR_X:
-            for dc in (1, 0):
-                if skip_self and dx == 0 and dc == 0:
-                    continue
-                x, core = (place.x + dx) % 4, (place.core + dc) % 2
-                body(y, place.turn_of(x, y, core), place.frame_of(x, y, core))
-
+def row_of(place, y):
+    frame, space, slot, start = y // 2 * 8, place.base + y % 2, y % 2 * HALF + y // 2 * 8, 25 * y
+    peers = []
+    for x in place.xs:
+        first = start + 6 * ((x + y) % 4)
+        for core in place.cores:
+            at = 2 * x + core
+            peers.append(Peer(frame + at, space, slot + at, first + 3 * core))
+    extra = (7 - y) % 4 * 2 + 1
+    return peers, Peer(frame + extra, space, slot + extra, start + 21)
+
+
+def for_peers(place, body, each_row=None):
     @pl.loop(0, 7)
     def _(a):
         dy = (1 - a % 2) * (4 + a // 2) + a % 2 * (4 - (a + 1) // 2)
-        y = (place.y + dy) % 8
-        one_y(y, False)
-        if each_y is not None:
-            each_y(y)
-
-    one_y(place.y, True)
-    if each_y is not None:
+        peers, extra = row_of(place, (place.y + dy) % 8)
+        for peer in peers:
+            body(peer)
+        if each_row is not None:
+            each_row(extra)
+
+    peers, extra = row_of(place, place.y)
+    for peer in peers[:-1]:
+        body(peer)
+    if each_row is not None:
 
         @pl.when(place.turn != 7)
         def _():
-            each_y(place.y)
+            each_row(extra)
 
 
 def by_turn(place, body):
@@ -120,8 +117,8 @@
 
 def kernel(
     image, maps, measured, lines, weights, noise, row_table, time_table,
-    out,
-    send, ret, recv, back, below, above, planes, noise_planes, raw_maps, coil_planes, lines_planes,
+    ret, known,
+    send, recv, back, below, above, planes, noise_planes, raw_maps, coil_planes, lines_planes,
     line_buf, weight_buf, row_buf, time_buf, back_table, spectra, moved, total, result,
     load_sem, own_sem, fwd_send, fwd_recv, ret_send, ret_recv, z_send, z_recv,
 ):
@@ -139,9 +136,8 @@
         [pltpu.make_async_copy(measured.at[f, 0, :, :, i, :], lines_planes.at[f, :, i], load_sem.at[4]) for f in range(2) for i in range(2)],
         [pltpu.make_async_copy(noise.at[f, 0, :, i, :], noise_planes.at[f, i], load_sem.at[5]) for f in range(2) for i in range(2)],
     ]
-    for group in loads:
-        for copy in group:
-            copy.start()
+    for copy in loads[1] + loads[0]:
+        copy.start()
 
     def finish(which):
         for copy in loads[which]:
@@ -149,10 +145,13 @@
 
     barrier = pltpu.get_barrier_semaphore()
 
-    def greet(y, turn, frame):
-        pl.semaphore_signal(barrier, inc=1, device_id=place.device(y, frame), device_id_type=MESH)
+    def greet(peer):
+        pl.semaphore_signal(barrier, inc=1, device_id=peer.device, device_id_type=MESH)
 
     for_peers(place, greet)
+    for group in loads[2:]:
+        for copy in group:
+            copy.start()
 
     @pl.when(place.z < 7)
     def _():
@@ -186,19 +185,18 @@
 
     for k in range(3):
 
-        def send_fwd(y, turn, frame):
+        def send_fwd(peer):
             pltpu.make_async_remote_copy(
-                send.at[pl.ds(place.start_of(y, turn) + k, 1)],
+                send.at[pl.ds(peer.start + k, 1)],
                 recv.at[pl.ds(k, 1), place.slot],
-                fwd_send, fwd_recv.at[k], device_id=place.device(y, frame), device_id_type=MESH,
+                fwd_send, fwd_recv.at[k], device_id=peer.device, device_id_type=MESH,
             ).start()
 
-        def send_extra(y):
-            frame = place.frame_of((7 - y) % 4, y, 1)
+        def send_extra(peer):
             pltpu.make_async_remote_copy(
-                send.at[pl.ds(25 * y + 24, 1)],
+                send.at[pl.ds(peer.start + 3, 1)],
                 recv.at[pl.ds(3, 1), place.slot],
-                fwd_send, fwd_recv.at[2], device_id=place.device(y, frame), device_id_type=MESH,
+                fwd_send, fwd_recv.at[2], device_id=peer.device, device_id_type=MESH,
             ).start()
 
         for_peers(place, send_fwd, send_extra if k == 2 else None)
@@ -318,11 +316,11 @@
             for g in range(k, k + count):
                 rows_out[span(HALF, g), :] += 0.125 * rows_above[pl.ds(4 * HALF * g, 4 * HALF), :]
 
-        def send_back(y, turn, frame):
+        def send_back(peer):
             pltpu.make_async_remote_copy(
-                back.at[pl.ds(k, count), place.slot_of(y, frame)],
+                back.at[pl.ds(k, count), peer.slot],
                 ret.at[pl.ds(place.start + k, count)],
-                ret_send, ret_recv, device_id=place.device(y, frame), device_id_type=MESH,
+                ret_send, ret_recv, device_id=peer.device, device_id_type=MESH,
             ).start()
 
         for_peers(place, send_back)
@@ -339,6 +337,8 @@
     to_lines(1)
     to_residual(1)
     to_image(1)
+    keep = pltpu.make_async_copy(result, known, load_sem.at[0])
+    keep.start()
 
     def settle(count):
         copy = pltpu.make_async_copy(back.at[pl.ds(0, count), place.slot], ret.at[pl.ds(place.start, count)], own_sem)
@@ -348,13 +348,6 @@
 
     by_turn(place, settle)
 
-    for f in range(2):
-        for i in range(2):
-            out[f, 0, :, i, 0:MAIN] = result[f, i, :, 0:MAIN] + ret[pl.ds(0, ROWS), f, i, :]
-            tails = ret[pl.ds(ROWS, 40), f, i, :]
-            tails = jnp.concatenate([tails[:, 32 * b : 32 * b + 32] for b in range(4)], axis=0)
-            out[f, 0, :, i, MAIN:COLS] = result[f, i, :, MAIN:COLS] + tails
-
     def drain(count):
         wait_bytes(send.at[pl.ds(0, GROUPS - count)], fwd_send)
         wait_bytes(recv.at[pl.ds(0, count), pl.ds(0, PEERS - 1)], ret_send)
@@ -371,19 +364,27 @@
                 down_copy(k, groups).wait_send()
 
     by_turn(place, drain)
+    keep.wait()
+
+
+def assemble(ret, known, out):
+    for i in range(2):
+        out[0, 0, :, i, 0:MAIN] = known[0, i, :, 0:MAIN] + ret[pl.ds(0, ROWS), 0, i, :]
+        tails = ret[pl.ds(ROWS, 40), 0, i, :]
+        tails = jnp.concatenate([tails[:, 32 * b : 32 * b + 32] for b in range(4)], axis=0)
+        out[0, 0, :, i, MAIN:COLS] = known[0, i, :, MAIN:COLS] + tails
 
 
 def on_device(image, maps, measured, lines, weights, noise):
     dma = pltpu.SemaphoreType.DMA
     anywhere = pl.BlockSpec(memory_space=pl.ANY)
-    return pl.pallas_call(
+    ret, known = pl.pallas_call(
         kernel,
         name="langevin_step",
-        out_shape=jax.ShapeDtypeStruct(image.shape, F32),
+        out_shape=(jax.ShapeDtypeStruct((GROUPS, 2, 2, MAIN), F32), jax.ShapeDtypeStruct((2, 2, ROWS, COLS), F32)),
         in_specs=[anywhere] * 8,
-        out_specs=pl.BlockSpec(memory_space=pltpu.VMEM),
+        out_specs=(anywhere, anywhere),
         scratch_shapes=[
-            pltpu.VMEM((GROUPS, 2, 2, MAIN), F32),
             pltpu.VMEM((GROUPS, 2, 2, MAIN), F32),
             pltpu.VMEM((4, PEERS, 2, 2, MAIN), F32),
             pltpu.VMEM((4, PEERS, 2, 2, MAIN), F32),
@@ -408,6 +409,18 @@
         compiler_params=pltpu.CompilerParams(collective_id=0, has_side_effects=True, vmem_limit_bytes=60 << 20),
         cost_estimate=pl.CostEstimate(flops=2_000_000_000, bytes_accessed=6_000_000, transcendentals=60_000),
     )(image, maps, measured, lines, weights.reshape(1, FRAMES), noise, jnp.asarray(row_tables()), jnp.asarray(time_tables()))
+    return pl.pallas_call(
+        assemble,
+        name="assemble",
+        out_shape=jax.ShapeDtypeStruct(image.shape, F32),
+        grid=(2,),
+        in_specs=[
+            pl.BlockSpec((GROUPS, 1, 2, MAIN), lambda f: (0, f, 0, 0)),
+            pl.BlockSpec((1, 2, ROWS, COLS), lambda f: (f, 0, 0, 0)),
+        ],
+        out_specs=pl.BlockSpec((1, 1, ROWS, 2, COLS), lambda f: (f, 0, 0, 0, 0)),
+        compiler_params=pltpu.CompilerParams(vmem_limit_bytes=60 << 20),
+    )(ret, known)
 
 
 def solution(mesh):

time: 37.8 us -> 36.8 us (0.974)
  local copies, waits for them, and re-layouts: 2.15 us -> 0 us
  Pallas kernels: 35.5 us -> 36.6 us
    unnamed x1 -> x0, local copies, waits for them, and re-layouts: 2.15 us -> none
    pallas_call x1 -> x2, Pallas kernels: 35.5 us -> 36.6 us  [the longest x1 34.1 us: on_device(): pl.pallas_call(kernel, name='langevin_step', out_shape=(jax.ShapeDtypeStr...]
where the time goes in v3:
time: 36.8 us; the launch traced here: 36.6 us
  Pallas kernels  36.6 us (99%)
    pallas_call x1, Pallas kernels, on_device(): pl.pallas_call(kernel, name='langevin_step', out_shape=(jax.ShapeDtypeStr...  34.1 us
    pallas_call x1, Pallas kernels, on_device(): pl.pallas_call(assemble, name='assemble', out_shape=jax.ShapeDtypeStruct(...  2.48 us

profile of v3, /device:TPU:1, one launch (start us, length us, event | category | flops | bytes accessed | tf_op | source)
XLA Modules:
  0.0 36.6 jit_solution(16465583311959729255)
XLA Ops:
  0.0 34.1 %langevin_step.1 = (f32[200,2,2,128]{3,2,1,0:T(2,128)}, f32[2,2,160,160]{3,2,1,0:T(8,128)}) custom-call(f32[2,1,160,2,160]{4,3,2,1,0:T(2,128)} %image.1, bf16[1,8,160,2,160]{4,3,2,1,0:T(2,128)(2,1)} %maps.1, f32[2,1,8,40,2,160]{5,4,3,2,1,0:T(2,128)} %measured.1, s32[2,40]{1,0:T(2,128)} %lines.1, f32[1,64]{1,0:T(1,128)} %bitcast.1, ...), custom_call_target="tpu_custom_call" | custom-call | flops 2000000000 | bytes 6000000 | tf_op jit(solution)/shard_map/langevin_step/pallas_call | solution.py:381
  34.1 2.5 %assemble.1 = f32[2,1,160,2,160]{4,3,2,1,0:T(2,128)} custom-call(f32[200,2,2,128]{3,2,1,0:T(2,128)} %get-tuple-element.7.ret, f32[2,2,160,160]{3,2,1,0:T(8,128)} %get-tuple-element.8.known), custom_call_target="tpu_custom_call" | custom-call | tf_op jit(solution)/shard_map/assemble/pallas_call | solution.py:412

commit v4 on v3

--- a/solution.py
+++ b/solution.py
@@ -81,24 +81,27 @@
     return peers, Peer(frame + extra, space, slot + extra, start + 21)
 
 
+def distance(a):
+    return (1 - a % 2) * (4 + a // 2) + a % 2 * (4 - (a + 1) // 2)
+
+
 def for_peers(place, body, each_row=None):
     @pl.loop(0, 7)
     def _(a):
-        dy = (1 - a % 2) * (4 + a // 2) + a % 2 * (4 - (a + 1) // 2)
-        peers, extra = row_of(place, (place.y + dy) % 8)
+        peers, extra = row_of(place, (place.y + distance(a)) % 8)
         for peer in peers:
-            body(peer)
+            body(peer, a)
         if each_row is not None:
-            each_row(extra)
+            each_row(extra, a)
 
     peers, extra = row_of(place, place.y)
     for peer in peers[:-1]:
-        body(peer)
+        body(peer, 7)
     if each_row is not None:
 
         @pl.when(place.turn != 7)
         def _():
-            each_row(extra)
+            each_row(extra, 7)
 
 
 def by_turn(place, body):
@@ -145,7 +148,7 @@
 
     barrier = pltpu.get_barrier_semaphore()
 
-    def greet(peer):
+    def greet(peer, a):
         pl.semaphore_signal(barrier, inc=1, device_id=peer.device, device_id_type=MESH)
 
     for_peers(place, greet)
@@ -185,18 +188,18 @@
 
     for k in range(3):
 
-        def send_fwd(peer):
+        def send_fwd(peer, a):
             pltpu.make_async_remote_copy(
                 send.at[pl.ds(peer.start + k, 1)],
                 recv.at[pl.ds(k, 1), place.slot],
-                fwd_send, fwd_recv.at[k], device_id=peer.device, device_id_type=MESH,
+                fwd_send, fwd_recv.at[k, a], device_id=peer.device, device_id_type=MESH,
             ).start()
 
-        def send_extra(peer):
+        def send_extra(peer, a):
             pltpu.make_async_remote_copy(
                 send.at[pl.ds(peer.start + 3, 1)],
                 recv.at[pl.ds(3, 1), place.slot],
-                fwd_send, fwd_recv.at[2], device_id=peer.device, device_id_type=MESH,
+                fwd_send, fwd_recv.at[2, a], device_id=peer.device, device_id_type=MESH,
             ).start()
 
         for_peers(place, send_fwd, send_extra if k == 2 else None)
@@ -263,15 +266,15 @@
     spot = (lax.broadcasted_iota(jnp.int32, (FRAMES, FRAMES), 0) == lax.broadcasted_iota(jnp.int32, (FRAMES, FRAMES), 1))
     column = -0.5 * jnp.sum(jnp.where(spot, weight_buf[...], 0.0), axis=1, keepdims=True)
 
-    def up_copy(k, count):
+    def up_copy(k, count, slot=0, width=HALF):
         return pltpu.make_async_remote_copy(
-            recv.at[pl.ds(k, count), pl.ds(HALF, HALF)], below.at[pl.ds(k, count)],
+            recv.at[pl.ds(k, count), pl.ds(HALF + slot, width)], below.at[pl.ds(k, count), pl.ds(slot, width)],
             z_send.at[k, 0], z_recv.at[k, 0], device_id=(place.frame, place.space + 2), device_id_type=MESH,
         )
 
-    def down_copy(k, count):
+    def down_copy(k, count, slot=0, width=HALF):
         return pltpu.make_async_remote_copy(
-            recv.at[pl.ds(k, count), pl.ds(0, HALF)], above.at[pl.ds(k, count)],
+            recv.at[pl.ds(k, count), pl.ds(slot, width)], above.at[pl.ds(k, count), pl.ds(slot, width)],
             z_send.at[k, 1], z_recv.at[k, 1], device_id=(place.frame, place.space - 2), device_id_type=MESH,
         )
 
@@ -282,15 +285,22 @@
         return pl.ds(4 * (PEERS * g + first), 4 * HALF)
 
     def arrive(k, count):
-        wait_bytes(recv.at[pl.ds(k, count), pl.ds(0, PEERS - 1)], fwd_recv.at[k])
-
-        @pl.when(place.z < 7)
-        def _():
-            up_copy(k, count).start()
-
-        @pl.when(place.z > 0)
-        def _():
-            down_copy(k, count).start()
+        def hand_on(y):
+            @pl.when((y % 2 == 1) & (place.z < 7))
+            def _():
+                up_copy(k, count, y // 2 * 8, 8).start()
+
+            @pl.when((y % 2 == 0) & (place.z > 0))
+            def _():
+                down_copy(k, count, y // 2 * 8, 8).start()
+
+        @pl.loop(0, 7)
+        def _(a):
+            wait_bytes(recv.at[pl.ds(k, count), pl.ds(0, 8)], fwd_recv.at[k, a])
+            hand_on((place.y + 8 - distance(a)) % 8)
+
+        wait_bytes(recv.at[pl.ds(k, count), pl.ds(0, 7)], fwd_recv.at[k, 7])
+        hand_on(place.y)
 
         blocks = [(first, g) for first in (0, HALF) for g in range(k, k + count)]
         stack = jnp.concatenate([rows_in[span(first, g), :] for first, g in blocks], axis=1)
@@ -316,7 +326,7 @@
             for g in range(k, k + count):
                 rows_out[span(HALF, g), :] += 0.125 * rows_above[pl.ds(4 * HALF * g, 4 * HALF), :]
 
-        def send_back(peer):
+        def send_back(peer, a):
             pltpu.make_async_remote_copy(
                 back.at[pl.ds(k, count), peer.slot],
                 ret.at[pl.ds(place.start + k, count)],
@@ -328,8 +338,8 @@
     to_lines(0)
     arrive(0, 1)
     to_residual(0)
+    leave(0, 1)
     arrive(1, 1)
-    leave(0, 1)
     by_turn(place, lambda count: arrive(2, count - 2))
     leave(1, 1)
     to_image(0)
@@ -404,7 +414,7 @@
             pltpu.VMEM((COILS, 2 * LINES, COLS), F32),
             pltpu.VMEM((2, ROWS, COLS), F32),
             pltpu.VMEM((2, 2, ROWS, COLS), F32),
-            dma((6,)), dma, dma, dma((3,)), dma, dma, dma((3, 2)), dma((3, 2)),
+            dma((6,)), dma, dma, dma((3, 8)), dma, dma, dma((3, 2)), dma((3, 2)),
         ],
         compiler_params=pltpu.CompilerParams(collective_id=0, has_side_effects=True, vmem_limit_bytes=60 << 20),
         cost_estimate=pl.CostEstimate(flops=2_000_000_000, bytes_accessed=6_000_000, transcendentals=60_000),

time: 36.8 us -> 39.5 us (1.073)
  Pallas kernels: 36.6 us -> 39 us
    pallas_call x1, Pallas kernels: 34.1 us -> 36.5 us  [on_device(): pl.pallas_call(kernel, name='langevin_step', out_shape=(jax.ShapeDtypeStr...]
where the time goes in v4:
time: 39.5 us; the launch traced here: 39 us
  Pallas kernels  39 us (99%)
    pallas_call x1, Pallas kernels, on_device(): pl.pallas_call(kernel, name='langevin_step', out_shape=(jax.ShapeDtypeStr...  36.5 us
    pallas_call x1, Pallas kernels, on_device(): pl.pallas_call(assemble, name='assemble', out_shape=jax.ShapeDtypeStruct(...  2.48 us

profile of v4, /device:TPU:1, one launch (start us, length us, event | category | flops | bytes accessed | tf_op | source)
XLA Modules:
  0.0 39.0 jit_solution(14837344230570096601)
XLA Ops:
  0.0 36.5 %langevin_step.1 = (f32[200,2,2,128]{3,2,1,0:T(2,128)}, f32[2,2,160,160]{3,2,1,0:T(8,128)}) custom-call(f32[2,1,160,2,160]{4,3,2,1,0:T(2,128)} %image.1, bf16[1,8,160,2,160]{4,3,2,1,0:T(2,128)(2,1)} %maps.1, f32[2,1,8,40,2,160]{5,4,3,2,1,0:T(2,128)} %measured.1, s32[2,40]{1,0:T(2,128)} %lines.1, f32[1,64]{1,0:T(1,128)} %bitcast.1, ...), custom_call_target="tpu_custom_call" | custom-call | flops 2000000000 | bytes 6000000 | tf_op jit(solution)/shard_map/langevin_step/pallas_call | solution.py:391
  36.5 2.5 %assemble.1 = f32[2,1,160,2,160]{4,3,2,1,0:T(2,128)} custom-call(f32[200,2,2,128]{3,2,1,0:T(2,128)} %get-tuple-element.7.ret, f32[2,2,160,160]{3,2,1,0:T(8,128)} %get-tuple-element.8.known), custom_call_target="tpu_custom_call" | custom-call | tf_op jit(solution)/shard_map/assemble/pallas_call | solution.py:422
